TPU v7x, 32 devices: a whole 2x2x4 slice. The times are simulated.
32 devices in a mesh: region: 4 (over y, core), seq: 8 (over z, x).
Axes of the slice: x: 2, y: 2, z: 4, core: 2. Of those that a mesh axis runs over, the one named last changes fastest.
Arguments:
- scan_tokens: bfloat16 [32768, 1024], P(('region', 'seq')), may hold values from -6 to 6
- grid_tokens: bfloat16 [8192, 1024], P(('region', 'seq')), may hold values from -6 to 6
- seg_slot: int32 [256], P(('region', 'seq')), may hold values from 0 to 255, as said below
- segment_lists: int32 [64, 8], P(('region', 'seq')), may hold values from 0 to 255, as said below
- query_weight: bfloat16 [1024, 1024], replicated, may hold values from -4 to 4
- key_weight: bfloat16 [1024, 1024], replicated, may hold values from -4 to 4
- value_weight: bfloat16 [1024, 1024], replicated, may hold values from -0.1875 to 0.1875
- mixer_weight: bfloat16 [1024, 1024], replicated, may hold values from -0.1875 to 0.1875
- packed_weight: bfloat16 [1024, 3072], replicated, may hold values from -4 to 4
- merged_weight: bfloat16 [1024, 1024], replicated, may hold values from -0.1875 to 0.1875
Outputs:
- encoded: bfloat16 [8192, 1024], P(('region', 'seq'))
Inputs may be any that keep to these rules, and one draw needn't show every extreme that they name: `seg_slot`: A permutation: each of the 256 segment slots holds exactly one segment. `segment_lists`: the 8 segments of a query block are held by 8 different devices, all of the block's own region (the devices that share the block's device's index along region); so the blocks of one device name at most 2 segments held by any one device, and in every draw and every region some device holds a segment of every query block of that region.
All inputs are finite; a program needn't handle non-finite values.
Results may differ from a plain program's by a relative error of at most 0.01.
The roundings to bfloat16 on the way count: a program that leaves them out, or rounds other values in their place, can miss the bound.
Values may be sent and summed in bfloat16 or wider, within the bound.
A program may use at most 128 MiB of HBM per device.

v0:
```python
import math

import jax
import jax.numpy as jnp
from jax import lax
from jax.sharding import PartitionSpec as P

H = 16
SEG = 128


norm_eps = 1e-06
masked_score = -1e30


def rms_rows(values):
    widened = values.astype(jnp.float32)
    scaled = widened / jnp.sqrt(jnp.mean(widened * widened, axis=-1, keepdims=True) + norm_eps)
    return scaled.astype(jnp.bfloat16)


def pair_partials(queries, seg_keys, seg_values, head_count):
    pair_count, query_rows, model_width = queries.shape
    key_rows = seg_keys.shape[1]
    head_dim = model_width // head_count
    q_split = queries.reshape(pair_count, query_rows, head_count, head_dim)
    k_split = seg_keys.reshape(pair_count, key_rows, head_count, head_dim)
    v_split = seg_values.reshape(pair_count, key_rows, head_count, head_dim)
    logit_scores = jnp.einsum(
        "bqhd,bkhd->bhqk", q_split, k_split, preferred_element_type=jnp.float32
    ) * (1.0 / math.sqrt(head_dim))
    maxima = jnp.max(logit_scores, axis=-1)
    weights = jnp.exp(logit_scores - maxima[..., None])
    running_sums = jnp.sum(weights, axis=-1)
    numerator = jnp.einsum(
        "bhqk,bkhd->bqhd", weights.astype(jnp.bfloat16), v_split, preferred_element_type=jnp.float32
    )
    return (numerator.reshape(pair_count, query_rows, model_width), maxima, running_sums)


def joined_pair_list(numerator, maxima, running_sums, live_pairs, head_count):
    live_mask = live_pairs[:, :, None, None]
    maxima = jnp.where(live_mask, maxima, masked_score)
    top_score = jnp.max(maxima, axis=0)
    factors = jnp.where(live_mask, jnp.exp(maxima - top_score[None]), 0.0)
    denominator = jnp.sum(factors * running_sums, axis=0)
    pair_count, block_count, query_rows, model_width = numerator.shape
    split_heads = numerator.reshape(
        pair_count, block_count, query_rows, head_count, model_width // head_count
    )
    summed = jnp.sum(split_heads * jnp.swapaxes(factors, 2, 3)[..., None], axis=0)
    merged = summed / jnp.swapaxes(denominator, 1, 2)[..., None]
    return merged.reshape(block_count, query_rows, model_width).astype(jnp.bfloat16)


def region_attention(packed, heads_local, head_dim):
    row_count = packed.shape[0]
    queries = packed[:, :, 0]
    head_keys = packed[:, :, 1]
    head_values = packed[:, :, 2]
    step_rows = min(512, row_count)

    def one_block(query_part):
        logit_scores = jnp.einsum(
            "qhd,khd->hqk", query_part, head_keys, preferred_element_type=jnp.float32
        ) * (1.0 / math.sqrt(head_dim))
        maxima = jnp.max(logit_scores, axis=-1, keepdims=True)
        weights = jnp.exp(logit_scores - maxima)
        running_sums = jnp.sum(weights, axis=-1)
        numerator = jnp.einsum(
            "hqk,khd->qhd",
            weights.astype(jnp.bfloat16),
            head_values,
            preferred_element_type=jnp.float32,
        )
        return (numerator / jnp.transpose(running_sums)[..., None]).astype(jnp.bfloat16)

    blocks = lax.map(
        one_block, queries.reshape(row_count // step_rows, step_rows, heads_local, head_dim)
    )
    return blocks.reshape(row_count, heads_local * head_dim)


def project_rows(rows, weight):
    return jnp.dot(rows, weight, preferred_element_type=jnp.float32).astype(jnp.bfloat16)


def on_device(
    scan_tokens,
    grid_tokens,
    seg_slot,
    segment_lists,
    query_weight,
    key_weight,
    value_weight,
    mixer_weight,
    packed_weight,
    merged_weight,
):
    seq_count = lax.axis_size("seq")
    head_count = H
    model_width = scan_tokens.shape[1]
    head_dim = model_width // head_count
    seg_local = scan_tokens.shape[0] // SEG
    block_local = segment_lists.shape[0]
    query_rows = grid_tokens.shape[0] // block_local
    all_slots = lax.all_gather(seg_slot, ("region", "seq"), axis=0, tiled=True)
    region_base = lax.axis_index("region") * (seq_count * seg_local)
    in_region = jnp.take(all_slots, segment_lists, axis=0) - region_base
    wanted = lax.all_gather(in_region, "seq", axis=0, tiled=True)
    own_index = lax.axis_index("seq")
    is_mine = wanted // seg_local == own_index
    pick_slot = jnp.sum(jnp.where(is_mine, wanted % seg_local, 0), axis=-1).reshape(
        seq_count, block_local
    )
    owner_ids = jnp.arange(seq_count, dtype=jnp.int32)
    live_pairs = jnp.any((in_region // seg_local)[None] == owner_ids[:, None, None], axis=-1)
    queries = jnp.dot(
        rms_rows(grid_tokens), query_weight, preferred_element_type=jnp.float32
    ).astype(jnp.bfloat16)
    queries = queries.reshape(block_local, query_rows, model_width)

    def attend_local(element):
        return pair_partials(queries, element[0], element[1], head_count)

    raw_segments = scan_tokens.reshape(seg_local, SEG, model_width)
    sent_raw = jnp.take(raw_segments, pick_slot, axis=0)
    got_raw = lax.all_to_all(sent_raw, "seq", split_axis=0, concat_axis=0, tiled=True)
    flat_raw = rms_rows(got_raw.reshape(-1, model_width))
    got_keys = project_rows(flat_raw, key_weight).reshape(seq_count, block_local, SEG, model_width)
    got_values = project_rows(flat_raw, value_weight).reshape(
        seq_count, block_local, SEG, model_width
    )
    numerator, maxima, running_sums = lax.map(attend_local, (got_keys, got_values))
    cross = joined_pair_list(numerator, maxima, running_sums, live_pairs, head_count).reshape(
        grid_tokens.shape[0], model_width
    )
    mixed = (
        grid_tokens.astype(jnp.float32)
        + jnp.dot(cross, mixer_weight, preferred_element_type=jnp.float32)
    ).astype(jnp.bfloat16)
    packed = jnp.dot(rms_rows(mixed), packed_weight, preferred_element_type=jnp.float32).astype(
        jnp.bfloat16
    )
    regional = lax.all_to_all(packed, "seq", split_axis=1, concat_axis=0, tiled=True)
    heads_local = head_count // seq_count
    attended = region_attention(
        regional.reshape(regional.shape[0], heads_local, 3, head_dim), heads_local, head_dim
    )
    returned = lax.all_to_all(attended, "seq", split_axis=0, concat_axis=1, tiled=True)
    return (
        mixed.astype(jnp.float32)
        + jnp.dot(returned, merged_weight, preferred_element_type=jnp.float32)
    ).astype(jnp.bfloat16)


def solution(mesh):
    in_specs = (
        P(("region", "seq"), None),
        P(("region", "seq"), None),
        P(("region", "seq")),
        P(("region", "seq"), None),
        P(),
        P(),
        P(),
        P(),
        P(),
        P(),
    )
    out_specs = P(("region", "seq"), None)
    return jax.shard_map(
        on_device, mesh=mesh, in_specs=in_specs, out_specs=out_specs, check_vma=False
    )
```

profile of v0, /device:TPU:2, one launch (start us, length us, event | category | flops | bytes accessed | tf_op | source)
XLA Modules:
  0.0 329.8 jit_solution(9341077791003331189)
XLA Ops:
  0.0 1.0 dynamic-update-slice
  1.0 41.3 %all-reduce = s32[256]{0:T(256)S(1)} all-reduce(s32[256]{0:T(256)S(1)} %dynamic-update-slice), channel_id=1, replica_groups=mesh['region'=4,'seq'=8] {'region','seq'}, use_global_device_ids=true, to_apply=%add | all-reduce | flops 256 | bytes 2048
  43.9 0.7 and_select_fusion
  44.6 16.0 %all-gather = s32[8,2,8]{2,1,0:T(2,128)S(1)} all-gather(s32[1,2,8]{2,1,0:T(2,128)S(1)} %bitcast.157), channel_id=1, replica_groups=mesh['region'=4,'seq'=8] {'seq'}, dimensions={0}, use_global_device_ids=true | all-gather | bytes 576 | tf_op jit(solution)/shard_map/all_gather | solution.py:110
  61.0 2.7 gather_fusion.1
  63.7 4.6 %broadcast_select_fusion = bf16[8,2,128,1024]{3,2,1,0:T(8,128)(2,1)} fusion(bf16[8,2,128,1024]{3,2,1,0:T(8,128)(2,1)} %bitcast.146, pred[8,2]{1,0:T(8,128)(4,1)S(1)} %compare_and_fusion), kind=kLoop, calls=%fused_computation.38 | loop fusion | flops 2097152 | bytes 8388624 | tf_op jit(solution)/shard_map/jit(_take)/select_n | solution.py:127
  68.4 8.5 %all-to-all-start = ((bf16[8,2,128,1024]{3,2,1,0:T(8,128)(2,1)}), bf16[8,2,128,1024]{3,2,1,0:T(8,128)(2,1)}, u32[]{:S(2)}, u32[]{:S(2)}) async-start(bf16[8,2,128,1024]{3,2,1,0:T(8,128)(2,1)} %broadcast_select_fusion), calls=%async_computation | async-start | bytes 8388608 | tf_op jit(solution)/shard_map/all_to_all | solution.py:128
  77.0 2.4 convolution_convert_fusion.3
  80.0 84.4 %all-to-all-done = bf16[8,2,128,1024]{3,2,1,0:T(8,128)(2,1)} async-done(((bf16[8,2,128,1024]{3,2,1,0:T(8,128)(2,1)}), bf16[8,2,128,1024]{3,2,1,0:T(8,128)(2,1)}, u32[]{:S(2)}, u32[]{:S(2)}) %all-to-all-start) | async-done | bytes 4194336 | tf_op jit(solution)/shard_map/all_to_all | solution.py:128
  164.4 3.1 multiply_reduce_fusion.1
  167.5 3.4 %fusion.35 = bf16[2048,1024]{1,0:T(8,128)(2,1)S(1)} fusion(f32[2048]{0:T(1024)S(1)} %bitcast.155, bf16[8,2,128,1024]{3,2,1,0:T(8,128)(2,1)} %all-to-all-done), kind=kLoop, calls=%fused_computation.36 | loop fusion | flops 6291456 | bytes 8396800 | tf_op jit(solution)/shard_map/convert_element_type | solution.py:19
  170.9 6.0 %convolution_convert_fusion.2 = bf16[2048,1024]{1,0:T(8,128)(2,1)} fusion(bf16[2048,1024]{1,0:T(8,128)(2,1)S(1)} %fusion.35, bf16[1024,1024]{1,0:T(8,128)(2,1)S(1)} %copy-done.8), kind=kOutput, calls=%fused_computation.41 | convolution fusion | flops 4297064448 | bytes 10485760 | tf_op jit(solution)/shard_map/dot_general | solution.py:85
  176.9 6.0 %convolution_convert_fusion.1 = bf16[2048,1024]{1,0:T(8,128)(2,1)} fusion(bf16[2048,1024]{1,0:T(8,128)(2,1)S(1)} %fusion.35, bf16[1024,1024]{1,0:T(8,128)(2,1)S(1)} %copy-done.9), kind=kOutput, calls=%fused_computation.40 | convolution fusion | flops 4297064448 | bytes 10485760 | tf_op jit(solution)/shard_map/dot_general | solution.py:85
  183.0 43.2 %while.26 = (s32[]{:T(128)}, f32[8,2,128,1024]{2,3,1,0:T(8,128)}, f32[8,2,16,128]{3,2,1,0:T(8,128)S(1)}, f32[8,2,16,128]{3,2,1,0:T(8,128)S(1)}, bf16[8,2,128,102...) while((s32[]{:T(128)}, f32[8,2,128,1024]{2,3,1,0:T(8,128)}, ...), condition=%wide.wide.region_6.7_spmd, body=%wide.wide.region_3.6_spmd.sunk | while | flops 138403840 | bytes 19530400 | solution.py:134
  183.0 1.3 constant_dynamic-slice_fusion.7
  185.5 1.1 constant_dynamic-slice_fusion.6
  187.3 1.1 constant_dynamic-update-slice_fusion.3
  188.4 1.3 constant_dynamic-slice_fusion.7
  190.9 1.1 constant_dynamic-slice_fusion.6
  192.7 1.1 constant_dynamic-update-slice_fusion.3
  193.9 1.3 constant_dynamic-slice_fusion.7
  196.4 1.1 constant_dynamic-slice_fusion.6
  198.2 1.1 constant_dynamic-update-slice_fusion.3
  199.2 1.3 constant_dynamic-slice_fusion.7
  201.7 1.1 constant_dynamic-slice_fusion.6
  203.6 1.1 constant_dynamic-update-slice_fusion.3
  204.6 1.3 constant_dynamic-slice_fusion.7
  207.1 1.1 constant_dynamic-slice_fusion.6
  209.0 1.0 constant_dynamic-update-slice_fusion.3
  210.0 1.3 constant_dynamic-slice_fusion.7
  212.5 1.1 constant_dynamic-slice_fusion.6
  214.3 1.1 constant_dynamic-update-slice_fusion.3
  215.4 1.3 constant_dynamic-slice_fusion.7
  217.9 1.1 constant_dynamic-slice_fusion.6
  219.8 1.1 constant_dynamic-update-slice_fusion.3
  220.8 1.3 constant_dynamic-slice_fusion.7
  223.3 1.1 constant_dynamic-slice_fusion.6
  225.2 1.0 constant_dynamic-update-slice_fusion.3
  226.4 4.1 %fusion.34 = f32[2,128,1024]{1,2,0:T(8,128)S(1)} fusion(f32[8,2,128,1024]{2,3,1,0:T(8,128)} %get-tuple-element.71, f32[8,2,128,16]{2,3,1,0:T(8,128)S(1)} %get-tuple-element.165), kind=kLoop, calls=%fused_computation.34 | loop fusion | flops 3932160 | bytes 9568256 | tf_op jit(solution)/shard_map/reduce_sum | solution.py:51
  231.8 2.5 fusion.40
  234.3 0.8 copy-done.5
  235.1 4.6 %convolution_convert_fusion = bf16[256,3072]{1,0:T(8,128)(2,1)S(1)} fusion(bf16[1024,3072]{1,0:T(8,128)(2,1)} %param.22, bf16[256,1024]{1,0:T(8,128)(2,1)S(1)} %get-tuple-element.168, f32[256]{0:T(256)S(1)} %add_sqrt_fusion.1), kind=kOutput, calls=%fused_computation.39 | convolution fusion | flops 1612185600 | bytes 8389632 | tf_op jit(solution)/shard_map/dot_general | solution.py:142
  239.7 1.6 copy.63
  241.3 4.2 %all-to-all-start.1 = ((bf16[256,8,384]{0,2,1:T(8,128)(2,1)}), bf16[256,8,384]{0,2,1:T(8,128)(2,1)S(1)}, u32[]{:S(2)}, u32[]{:S(2)}) async-start(bf16[256,8,384]{0,2,1:T(8,128)(2,1)} %bitcast.23), calls=%async_computation.1 | async-start | bytes 3145728 | tf_op jit(solution)/shard_map/all_to_all | solution.py:145
  245.6 36.5 %all-to-all-done.1 = bf16[256,8,384]{0,2,1:T(8,128)(2,1)S(1)} async-done(((bf16[256,8,384]{0,2,1:T(8,128)(2,1)}), bf16[256,8,384]{0,2,1:T(8,128)(2,1)S(1)}, u32[]{:S(2)}, u32[]{:S(2)}) %all-to-all-start.1) | async-done | bytes 1572896 | tf_op jit(solution)/shard_map/all_to_all | solution.py:145
  282.1 0.9 copy.58
  283.0 0.8 reshape.154
  283.8 0.9 slice_bitcast_fusion
  285.2 21.4 %while.25 = (s32[]{:T(128)}, bf16[4,512,2,64]{1,3,2,0:T(8,128)(2,1)}, bf16[4,512,2,64]{1,3,2,0:T(8,128)(2,1)S(1)}, bf16[2048,2,64]{0,2,1:T(8,128)(2,1)S(1)}, bf16[2048,2,64]{0,2,1:T(8,128)(2,1)}, /*index=5*/s32[]{:T(128)}) while((s32[]{:T(128)}, bf16[4,512,2,64]{1,3,2,0:T(8,128)(2,1)}, bf16[4,512,2,64]{1,3,2,0:T(8,128)(2,1)S(1)}, ...), condition=%wide.region_15.16_spmd, body=%wide.region_12.15_spmd.sunk | while | flops 553777152 | bytes 28594788 | solution.py:78
  285.2 1.4 multiply_reduce_fusion.4
  286.6 1.6 fusion.88
  288.3 2.3 fusion.89
  290.6 1.4 multiply_reduce_fusion.4
  292.0 1.6 fusion.88
  293.6 2.3 fusion.89
  295.9 1.4 multiply_reduce_fusion.4
  297.3 1.6 fusion.88
  299.0 2.3 fusion.89
  301.3 1.4 multiply_reduce_fusion.4
  302.7 1.6 fusion.88
  304.3 2.3 fusion.89
  306.6 1.6 copy.60
  308.5 18.2 %all_to_all.40 = bf16[8,256,128]{1,2,0:T(8,128)(2,1)S(1)} all-to-all(bf16[8,256,128]{1,2,0:T(8,128)(2,1)S(1)} %copy.61), channel_id=1, replica_groups=mesh['region'=4,'seq'=8] {'seq'}, dimensions={0} | all-to-all | bytes 1048576 | tf_op jit(solution)/shard_map/all_to_all | solution.py:150
  326.6 3.2 fusion.37
  (138 shorter events, 20.3 us)
Async XLA Ops:
  0.0 61.0 %copy-start = (bf16[1024,1024]{1,0:T(8,128)(2,1)S(1)}, bf16[1024,1024]{1,0:T(8,128)(2,1)}, u32[]{:S(2)}) copy-start(bf16[1024,1024]{1,0:T(8,128)(2,1)} %param.14) | copy-start | bytes 6291460
  68.3 8.5 %copy-start.6 = (bf16[256,1024]{1,0:T(8,128)(2,1)S(1)}, bf16[256,1024]{1,0:T(8,128)(2,1)}, u32[]{:S(2)}) copy-start(bf16[256,1024]{1,0:T(8,128)(2,1)} %param.15) | copy-start | bytes 1572868
  68.4 96.0 %all-to-all-start = ((bf16[8,2,128,1024]{3,2,1,0:T(8,128)(2,1)}), bf16[8,2,128,1024]{3,2,1,0:T(8,128)(2,1)}, u32[]{:S(2)}, u32[]{:S(2)}) async-start(bf16[8,2,128,1024]{3,2,1,0:T(8,128)(2,1)} %broadcast_select_fusion), calls=%async_computation | async-start | bytes 8388608 | tf_op jit(solution)/shard_map/all_to_all | solution.py:128
  79.6 91.3 %copy-start.4 = (bf16[256,1024]{0,1:T(8,128)(2,1)}, bf16[256,1024]{0,1:T(8,128)(2,1)S(1)}, u32[]{:S(2)}) copy-start(bf16[256,1024]{0,1:T(8,128)(2,1)S(1)} %copy.52) | copy-start | bytes 1572868
  167.5 3.4 %copy-start.8 = (bf16[1024,1024]{1,0:T(8,128)(2,1)S(1)}, bf16[1024,1024]{1,0:T(8,128)(2,1)}, u32[]{:S(2)}) copy-start(bf16[1024,1024]{1,0:T(8,128)(2,1)} %param.20) | copy-start | bytes 6291460
  170.9 6.0 %copy-start.9 = (bf16[1024,1024]{1,0:T(8,128)(2,1)S(1)}, bf16[1024,1024]{1,0:T(8,128)(2,1)}, u32[]{:S(2)}) copy-start(bf16[1024,1024]{1,0:T(8,128)(2,1)} %param.19) | copy-start | bytes 6291460
  183.0 2.5 copy-start.2
  186.9 1.5 copy-start.3
  188.4 2.5 copy-start.2
  192.3 1.6 copy-start.3
  193.9 2.5 copy-start.2
  197.7 1.5 copy-start.3
  199.2 2.5 copy-start.2
  203.1 1.5 copy-start.3
  204.6 2.5 copy-start.2
  208.5 1.5 copy-start.3
  210.0 2.5 copy-start.2
  213.9 1.6 copy-start.3
  215.4 2.5 copy-start.2
  219.3 1.5 copy-start.3
  220.8 2.5 copy-start.2
  224.7 1.5 copy-start.3
  234.3 0.8 copy-start.5
  241.3 40.8 %all-to-all-start.1 = ((bf16[256,8,384]{0,2,1:T(8,128)(2,1)}), bf16[256,8,384]{0,2,1:T(8,128)(2,1)S(1)}, u32[]{:S(2)}, u32[]{:S(2)}) async-start(bf16[256,8,384]{0,2,1:T(8,128)(2,1)} %bitcast.23), calls=%async_computation.1 | async-start | bytes 3145728 | tf_op jit(solution)/shard_map/all_to_all | solution.py:145
  286.6 1.7 copy-start.7
  291.9 1.7 copy-start.7
  297.3 1.7 copy-start.7
  302.7 1.7 copy-start.7
  306.6 23.2 %copy-start.1 = (bf16[1024,1024]{1,0:T(8,128)(2,1)S(1)}, bf16[1024,1024]{1,0:T(8,128)(2,1)}, u32[]{:S(2)}) copy-start(bf16[1024,1024]{1,0:T(8,128)(2,1)} %param.14) | copy-start | bytes 6291460
where the time goes:
time: 333 us; the launch traced here: 330 us
  waiting for transfers between devices  121 us (36%)
  blocking collectives  75.5 us (23%)
  matrix products  47.4 us (14%)
  local copies, waits for them, and re-layouts  45.4 us (14%)
  other arithmetic  27.2 us (8%)
  starting transfers between devices  12.7 us (4%)
    all_to_all x1, waiting for transfers between devices, on_device(): lax.all_to_all(sent_raw, 'seq', split_axis=0, concat_axis=0, tiled=True)  84.4 us
    unnamed x1, blocking collectives  41.3 us
    all_to_all x1, waiting for transfers between devices, on_device(): lax.all_to_all(packed, 'seq', split_axis=1, concat_axis=0, tiled=True)  36.5 us
    dynamic_slice x32, local copies, waits for them, and re-layouts, on_device(): lax.map(attend_local, (got_keys, got_values))  23.1 us
    all_to_all x1, blocking collectives, on_device(): lax.all_to_all(attended, 'seq', split_axis=0, concat_axis=1, tiled=True)  18.2 us
    all_gather x1, blocking collectives, on_device(): wanted = lax.all_gather(in_region, 'seq', axis=0, tiled=True)  16 us
    dot_general x2, matrix products, project_rows(): jnp.dot(rows, weight, preferred_element_type=jnp.float32)  12 us
    dot_general x4, matrix products, one_block(): jnp.einsum('hqk,khd->qhd', weights.astype(jnp.bfloat16), head_values, pre...  9.23 us
  transfers between devices with their start and end apart: 2, of which 2 were waited for; matrix products, arithmetic and copies ran while one was open for 1% of the time, Pallas kernels for 0%

commit v1 on v0

v1 whole, which is shorter than its diff:
```python
import functools
import math

import jax
import jax.numpy as jnp
from jax import lax
from jax.experimental import pallas as pl
from jax.experimental.pallas import tpu as pltpu
from jax.sharding import PartitionSpec as P

H = 16
SEG = 128

norm_eps = 1e-06
masked_score = -1e30
MESH = pl.DeviceIdType.MESH
VMEM_BYTES = 56 * 1024 * 1024


def rms_f32(widened):
    return widened / jnp.sqrt(jnp.mean(widened * widened, axis=-1, keepdims=True) + norm_eps)


def rms_rows(values):
    return rms_f32(values.astype(jnp.float32)).astype(jnp.bfloat16)


def stride_for(count):
    return 3 if math.gcd(3, count) == 1 else 1


def index_kernel(n_reg, n_seq, in_ref, out_ref, send_sem, recv_sem, send_sem2, recv_sem2):
    reg, seq = lax.axis_index("region"), lax.axis_index("seq")
    barrier = pltpu.get_barrier_semaphore()
    for k in range(1, n_reg):
        pl.semaphore_signal(
            barrier, inc=1, device_id=(lax.rem(reg + k, n_reg), seq), device_id_type=MESH
        )
    for k in range(1, n_seq):
        pl.semaphore_signal(
            barrier, inc=1, device_id=(reg, lax.rem(seq + k, n_seq)), device_id_type=MESH
        )
    out_ref[seq, reg] = in_ref[...]
    pl.semaphore_wait(barrier, n_reg + n_seq - 2)

    def over_region(k):
        return pltpu.make_async_remote_copy(
            src_ref=in_ref,
            dst_ref=out_ref.at[seq, reg],
            send_sem=send_sem.at[k],
            recv_sem=recv_sem.at[k],
            device_id=(lax.rem(reg + k, n_reg), seq),
            device_id_type=MESH,
        )

    for k in range(1, n_reg):
        over_region(k).start()
    for k in range(1, n_reg):
        over_region(k).wait()

    def over_seq(k):
        return pltpu.make_async_remote_copy(
            src_ref=out_ref.at[seq],
            dst_ref=out_ref.at[seq],
            send_sem=send_sem2.at[k],
            recv_sem=recv_sem2.at[k],
            device_id=(reg, lax.rem(seq + k, n_seq)),
            device_id_type=MESH,
        )

    for k in range(1, n_seq):
        over_seq(k).start()
    for k in range(1, n_seq):
        over_seq(k).wait()


def gather_indices(packed, n_reg, n_seq):
    return pl.pallas_call(
        functools.partial(index_kernel, n_reg, n_seq),
        out_shape=jax.ShapeDtypeStruct((n_seq, n_reg) + packed.shape, jnp.int32),
        in_specs=[pl.BlockSpec(memory_space=pltpu.VMEM)],
        out_specs=pl.BlockSpec(memory_space=pltpu.VMEM),
        scratch_shapes=[
            pltpu.SemaphoreType.DMA((n_reg,)),
            pltpu.SemaphoreType.DMA((n_reg,)),
            pltpu.SemaphoreType.DMA((n_seq,)),
            pltpu.SemaphoreType.DMA((n_seq,)),
        ],
        compiler_params=pltpu.CompilerParams(collective_id=0, has_side_effects=True),
    )(packed)


def cross_kernel(
    n, blocks, pairs, head_dim, all_live,
    pick_ref, live_ref, scan_ref, grid_ref, wq_hbm, wk_hbm, wv_hbm,
    out_ref,
    wq, wk, wv, send, recv, qm, ks, vs, top, total, acc,
    w_sem, send_sem, recv_sem,
):
    reg, me = lax.axis_index("region"), lax.axis_index("seq")
    stride = stride_for(n)
    loads = [
        pltpu.make_async_copy(src, dst, w_sem.at[i])
        for i, (src, dst) in enumerate(((wq_hbm, wq), (wk_hbm, wk), (wv_hbm, wv)))
    ]
    for load in loads:
        load.start()
    barrier = pltpu.get_barrier_semaphore()
    for k in range(1, n):
        pl.semaphore_signal(
            barrier, inc=1, device_id=(reg, lax.rem(me + k, n)), device_id_type=MESH
        )
    pl.semaphore_wait(barrier, n - 1)

    def copy(i):
        return pltpu.make_async_remote_copy(
            src_ref=send.at[i],
            dst_ref=recv.at[i],
            send_sem=send_sem.at[i],
            recv_sem=recv_sem.at[i],
            device_id=(reg, lax.rem(me + stride * i, n)),
            device_id_type=MESH,
        )

    def stage(i, carry):
        for b in range(blocks):
            send[i, b * SEG : (b + 1) * SEG] = rms_rows(scan_ref[pick_ref[i, b]])
        copy(i).start()
        return carry

    lax.fori_loop(1, n, stage, 0)
    for b in range(blocks):
        recv[0, b * SEG : (b + 1) * SEG] = rms_rows(scan_ref[pick_ref[0, b]])

    rows = grid_ref.shape[0] // blocks
    width = 2 * head_dim
    low = lax.broadcasted_iota(jnp.int32, (rows, width), 1) < head_dim
    loads[0].wait()
    scale = 1.0 / math.sqrt(head_dim)
    queries = jnp.dot(rms_rows(grid_ref[...]), wq[...], preferred_element_type=jnp.float32)
    queries = queries.astype(jnp.bfloat16).astype(jnp.float32) * scale
    for b in range(blocks):
        for p in range(pairs):
            part = queries[b * rows : (b + 1) * rows, p * width : (p + 1) * width]
            j = b * pairs + p
            qm[j, :rows] = jnp.where(low, part, 0.0).astype(jnp.bfloat16)
            qm[j, rows:] = jnp.where(low, 0.0, part).astype(jnp.bfloat16)
    top[...] = jnp.full(top.shape, masked_score, jnp.float32)
    total[...] = jnp.zeros(total.shape, jnp.float32)
    acc[...] = jnp.zeros(acc.shape, jnp.float32)
    for p in range(pairs):
        vs[p, :, width:] = jnp.ones((blocks * SEG, width), jnp.bfloat16)
    loads[1].wait()
    loads[2].wait()

    def process(i, carry):
        @pl.when(i > 0)
        def _():
            copy(i).wait_recv()

        arrived = recv[i]
        keys = jnp.dot(arrived, wk[...], preferred_element_type=jnp.float32).astype(jnp.bfloat16)
        for p in range(pairs):
            ks[p] = keys[:, p * width : (p + 1) * width]
        vals = jnp.dot(arrived, wv[...], preferred_element_type=jnp.float32).astype(jnp.bfloat16)
        for p in range(pairs):
            vs[p, :, :width] = vals[:, p * width : (p + 1) * width]

        for b in range(blocks):
            at = slice(b * SEG, (b + 1) * SEG)

            def attend(p, b, at):
                j = b * pairs + p
                scores = lax.dot_general(
                    qm[j], ks[p, at], (((1,), (1,)), ((), ())), preferred_element_type=jnp.float32
                )
                if not all_live:
                    scores = jnp.where(live_ref[i, b] > 0, scores, masked_score)
                old = top[j]
                new = jnp.maximum(old, jnp.max(scores, axis=-1, keepdims=True))
                weights = jnp.exp(scores - new).astype(jnp.bfloat16)
                factor = jnp.exp(old - new)
                factor = jnp.where(low, factor[:rows], factor[rows:])
                summed = jnp.dot(weights, vs[p, at], preferred_element_type=jnp.float32)
                acc[j] = acc[j] * factor + jnp.where(low, summed[:rows, :width], summed[rows:, :width])
                total[j] = total[j] * factor + jnp.where(
                    low, summed[:rows, width:], summed[rows:, width:]
                )
                top[j] = new

            def four(g, inner, b=b, at=at):
                for u in range(4):
                    attend(g * 4 + u, b, at)
                return inner

            lax.fori_loop(0, pairs // 4, four, 0)
        return carry

    lax.fori_loop(0, n, process, 0)
    for b in range(blocks):
        for p in range(pairs):
            j = b * pairs + p
            out_ref[b * rows : (b + 1) * rows, p * width : (p + 1) * width] = (
                acc[j] / total[j]
            ).astype(jnp.bfloat16)

    def finish(i, carry):
        copy(i).wait_send()
        return carry

    lax.fori_loop(1, n, finish, 0)


def cross_attention(pick, live, scan, grid_tokens, wq, wk, wv, n, blocks, all_live):
    rows, model = grid_tokens.shape
    head_dim = model // H
    pairs = H // 2
    width = 2 * head_dim
    block_rows = rows // blocks
    vmem = pl.BlockSpec(memory_space=pltpu.VMEM)
    smem = pl.BlockSpec(memory_space=pltpu.SMEM)
    hbm = pl.BlockSpec(memory_space=pl.ANY)
    weight = pltpu.VMEM((model, model), jnp.bfloat16)
    return pl.pallas_call(
        functools.partial(cross_kernel, n, blocks, pairs, head_dim, all_live),
        out_shape=jax.ShapeDtypeStruct((rows, model), jnp.bfloat16),
        in_specs=[smem, smem, vmem, vmem, hbm, hbm, hbm],
        out_specs=vmem,
        scratch_shapes=[
            weight,
            weight,
            weight,
            pltpu.VMEM((n, blocks * SEG, model), jnp.bfloat16),
            pltpu.VMEM((n, blocks * SEG, model), jnp.bfloat16),
            pltpu.VMEM((blocks * pairs, 2 * block_rows, width), jnp.bfloat16),
            pltpu.VMEM((pairs, blocks * SEG, width), jnp.bfloat16),
            pltpu.VMEM((pairs, blocks * SEG, 2 * width), jnp.bfloat16),
            pltpu.VMEM((blocks * pairs, 2 * block_rows, SEG), jnp.float32),
            pltpu.VMEM((blocks * pairs, block_rows, width), jnp.float32),
            pltpu.VMEM((blocks * pairs, block_rows, width), jnp.float32),
            pltpu.SemaphoreType.DMA((3,)),
            pltpu.SemaphoreType.DMA((n,)),
            pltpu.SemaphoreType.DMA((n,)),
        ],
        compiler_params=pltpu.CompilerParams(
            collective_id=1, has_side_effects=True, vmem_limit_bytes=VMEM_BYTES
        ),
    )(pick, live, scan, grid_tokens, wq, wk, wv)


def region_kernel(
    n, heads, head_dim, packed_ref, out_ref,
    took, ks, vs, made, got, send_sem, recv_sem, send_sem2, recv_sem2,
):
    reg, me = lax.axis_index("region"), lax.axis_index("seq")
    stride = stride_for(n)
    rows = packed_ref.shape[1]
    barrier = pltpu.get_barrier_semaphore()
    for k in range(1, n):
        pl.semaphore_signal(
            barrier, inc=1, device_id=(reg, lax.rem(me + k, n)), device_id_type=MESH
        )
    pl.semaphore_wait(barrier, n - 1)

    def outward(i):
        to = lax.rem(me + stride * i, n)
        return pltpu.make_async_remote_copy(
            src_ref=packed_ref.at[to],
            dst_ref=took.at[me],
            send_sem=send_sem.at[i],
            recv_sem=recv_sem.at[i],
            device_id=(reg, to),
            device_id_type=MESH,
        )

    def inward(i):
        source = lax.rem(me + (n * stride - stride * i), n)
        return pltpu.make_async_remote_copy(
            src_ref=packed_ref.at[source],
            dst_ref=took.at[source],
            send_sem=send_sem.at[i],
            recv_sem=recv_sem.at[i],
            device_id=(reg, source),
            device_id_type=MESH,
        )

    def back(i):
        to = lax.rem(me + stride * i, n)
        return pltpu.make_async_remote_copy(
            src_ref=made.at[i],
            dst_ref=got.at[me],
            send_sem=send_sem2.at[i],
            recv_sem=recv_sem2.at[i],
            device_id=(reg, to),
            device_id_type=MESH,
        )

    def back_in(i):
        source = lax.rem(me + (n * stride - stride * i), n)
        return pltpu.make_async_remote_copy(
            src_ref=made.at[i],
            dst_ref=got.at[source],
            send_sem=send_sem2.at[i],
            recv_sem=recv_sem2.at[i],
            device_id=(reg, source),
            device_id_type=MESH,
        )

    def each(first, last, body):
        def step(i, carry):
            body(i)
            return carry

        lax.fori_loop(first, last, step, 0)

    each(1, n, lambda i: outward(i).start())

    def place(source):
        part = took[source]
        at = pl.ds(pl.multiple_of(source * rows, rows), rows)
        for h in range(heads):
            base = 3 * h * head_dim
            ks[h, at, :] = part[:, base + head_dim : base + 2 * head_dim]
            vs[h, at, :head_dim] = part[:, base + 2 * head_dim : base + 3 * head_dim]

    for h in range(heads):
        vs[h, :, head_dim:] = jnp.ones((n * rows, head_dim), jnp.bfloat16)
    took[me] = packed_ref[me]
    place(me)

    def arrive(i):
        inward(i).wait_recv()
        place(lax.rem(me + (n * stride - stride * i), n))

    each(1, n, arrive)
    scale = 1.0 / math.sqrt(head_dim)

    def attend(i):
        to = lax.rem(me + stride * i, n)
        part = took[to]
        for h in range(heads):
            base = 3 * h * head_dim
            q = part[:, base : base + head_dim] * jnp.bfloat16(scale)
            scores = lax.dot_general(
                q, ks[h], (((1,), (1,)), ((), ())), preferred_element_type=jnp.float32
            )
            peak = jnp.max(scores, axis=-1, keepdims=True)
            weights = jnp.exp(scores - peak).astype(jnp.bfloat16)
            summed = jnp.dot(weights, vs[h], preferred_element_type=jnp.float32)
            made[i, :, h * head_dim : (h + 1) * head_dim] = (
                summed[:, :head_dim] / summed[:, head_dim:]
            ).astype(jnp.bfloat16)

    def attend_send(i):
        attend(i)
        back(i).start()

    each(1, n, attend_send)
    attend(0)
    got[me] = made[0]
    each(1, n, lambda i: back_in(i).wait_recv())
    span = heads * head_dim
    for s in range(n):
        out_ref[:, s * span : (s + 1) * span] = got[s]
    each(1, n, lambda i: outward(i).wait_send())
    each(1, n, lambda i: back(i).wait_send())


def region_attention(packed, n):
    _, rows, columns = packed.shape
    heads = H // n
    head_dim = columns // (3 * heads)
    span = heads * head_dim
    vmem = pl.BlockSpec(memory_space=pltpu.VMEM)
    return pl.pallas_call(
        functools.partial(region_kernel, n, heads, head_dim),
        out_shape=jax.ShapeDtypeStruct((rows, n * span), jnp.bfloat16),
        in_specs=[vmem],
        out_specs=vmem,
        scratch_shapes=[
            pltpu.VMEM((n, rows, columns), jnp.bfloat16),
            pltpu.VMEM((heads, n * rows, head_dim), jnp.bfloat16),
            pltpu.VMEM((heads, n * rows, 2 * head_dim), jnp.bfloat16),
            pltpu.VMEM((n, rows, span), jnp.bfloat16),
            pltpu.VMEM((n, rows, span), jnp.bfloat16),
            pltpu.SemaphoreType.DMA((n,)),
            pltpu.SemaphoreType.DMA((n,)),
            pltpu.SemaphoreType.DMA((n,)),
            pltpu.SemaphoreType.DMA((n,)),
        ],
        compiler_params=pltpu.CompilerParams(
            collective_id=2, has_side_effects=True, vmem_limit_bytes=VMEM_BYTES
        ),
    )(packed)


def on_device(
    scan_tokens,
    grid_tokens,
    seg_slot,
    segment_lists,
    query_weight,
    key_weight,
    value_weight,
    mixer_weight,
    packed_weight,
    merged_weight,
):
    n_reg, n = lax.axis_size("region"), lax.axis_size("seq")
    reg, me = lax.axis_index("region"), lax.axis_index("seq")
    model_width = scan_tokens.shape[1]
    seg_local = scan_tokens.shape[0] // SEG
    blocks, overlap = segment_lists.shape
    rows = grid_tokens.shape[0]

    flat = jnp.concatenate([seg_slot, segment_lists.reshape(-1)])
    used = flat.shape[0]
    tiles = -(-used // 1024)
    flat = jnp.pad(flat, (0, tiles * 1024 - used)).reshape(tiles * 8, 128)
    tables = gather_indices(flat, n_reg, n).reshape(n, n_reg, tiles * 1024)
    all_slots = jnp.swapaxes(tables[:, :, :seg_local], 0, 1).reshape(-1)
    lists = lax.dynamic_index_in_dim(tables, reg, axis=1, keepdims=False)
    lists = lists[:, seg_local:used].reshape(n, blocks, overlap)
    numbers = jnp.arange(all_slots.shape[0], dtype=jnp.int32)
    wanted = jnp.sum(jnp.where(lists[..., None] == numbers, all_slots, 0), axis=-1)
    wanted = wanted - reg * (n * seg_local)
    mine = wanted // seg_local == me
    pick = jnp.sum(jnp.where(mine, wanted % seg_local, 0), axis=-1)
    steps = stride_for(n) * jnp.arange(n, dtype=jnp.int32)
    pick = jnp.take(pick, (me + steps) % n, axis=0, mode="clip")
    all_live = overlap == n
    if all_live:
        live = jnp.ones((n, blocks), jnp.int32)
    else:
        own = lax.dynamic_index_in_dim(wanted, me, axis=0, keepdims=False) // seg_local
        sources = (me - steps) % n
        live = jnp.any(own[None] == sources[:, None, None], axis=-1).astype(jnp.int32)

    cross = cross_attention(
        pick, live, scan_tokens.reshape(seg_local, SEG, model_width), grid_tokens,
        query_weight, key_weight, value_weight, n, blocks, all_live,
    )
    mixed = (
        grid_tokens.astype(jnp.float32)
        + jnp.dot(cross, mixer_weight, preferred_element_type=jnp.float32)
    ).astype(jnp.bfloat16)
    packed = jnp.dot(rms_rows(mixed), packed_weight, preferred_element_type=jnp.float32).astype(
        jnp.bfloat16
    )
    returned = region_attention(jnp.swapaxes(packed.reshape(rows, n, -1), 0, 1), n)
    return (
        mixed.astype(jnp.float32)
        + jnp.dot(returned, merged_weight, preferred_element_type=jnp.float32)
    ).astype(jnp.bfloat16)


def solution(mesh):
    in_specs = (
        P(("region", "seq"), None),
        P(("region", "seq"), None),
        P(("region", "seq")),
        P(("region", "seq"), None),
        P(),
        P(),
        P(),
        P(),
        P(),
        P(),
    )
    out_specs = P(("region", "seq"), None)
    return jax.shard_map(
        on_device, mesh=mesh, in_specs=in_specs, out_specs=out_specs, check_vma=False
    )
```

time: 333 us -> 200 us (0.60)
  Pallas kernels: 0 us -> 178 us
  waiting for transfers between devices: 121 us -> 0 us
  blocking collectives: 75.5 us -> 0 us
  matrix products: 47.4 us -> 10.2 us
  local copies, waits for them, and re-layouts: 45.4 us -> 9.68 us
  other arithmetic: 27.2 us -> 1.43 us
  starting transfers between devices: 12.7 us -> 0 us
    pallas_call x0 -> x3, Pallas kernels: none -> 178 us  [the longest x1 104 us: cross_attention(): pl.pallas_call(functools.partial(cross_kernel, n, blocks, pairs, head_dim...]
    all_to_all x2 -> x0, waiting for transfers between devices: 121 us -> none  [the longest x1 84.4 us: on_device(): lax.all_to_all(sent_raw, 'seq', split_axis=0, concat_axis=0, tiled=True)]
    unnamed x1 -> x0, blocking collectives: 41.3 us -> none
    dot_general x27 -> x0, matrix products: 37.1 us -> none  [the longest x2 12 us: project_rows(): jnp.dot(rows, weight, preferred_element_type=jnp.float32)]
    dynamic_slice x32 -> x1, local copies, waits for them, and re-layouts: 23.1 us -> 0.04 us  [on_device(): lists = lax.dynamic_index_in_dim(tables, reg, axis=1, keepdims=False)]
    all_to_all x1 -> x0, blocking collectives: 18.2 us -> none  [on_device(): lax.all_to_all(attended, 'seq', split_axis=0, concat_axis=1, tiled=True)]
    reduce_sum x16 -> x2, other arithmetic: 17.2 us -> 0.67 us  [the longest x1 0.44 us: on_device(): jnp.sum(jnp.where(lists[..., None] == numbers, all_slots, 0), axis=-1)]
    all_gather x1 -> x0, blocking collectives: 16 us -> none  [on_device(): wanted = lax.all_gather(in_region, 'seq', axis=0, tiled=True)]
  transfers between devices with their start and end apart: 2 -> 0, of which waited for: 2 -> 0; matrix products, arithmetic and copies ran while one was open for 1% -> 0% of each run, Pallas kernels for 0% -> 0%
where the time goes in v1:
time: 200 us; the launch traced here: 199 us
  Pallas kernels  178 us (89%)
  matrix products  10.2 us (5%)
  local copies, waits for them, and re-layouts  9.68 us (5%)
    pallas_call x1, Pallas kernels, cross_attention(): pl.pallas_call(functools.partial(cross_kernel, n, blocks, pairs, head_dim...  104 us
    pallas_call x1, Pallas kernels, region_attention(): pl.pallas_call(functools.partial(region_kernel, n, heads, head_dim), out_...  61.2 us
    pallas_call x1, Pallas kernels, gather_indices(): pl.pallas_call(functools.partial(index_kernel, n_reg, n_seq), out_shape=j...  12.8 us
    dot_general x1, matrix products, on_device(): jnp.dot(rms_rows(mixed), packed_weight, preferred_element_type=jnp.float32)  5.79 us

profile of v1, /device:TPU:2, one launch (start us, length us, event | category | flops | bytes accessed | tf_op | source)
XLA Modules:
  0.0 199.1 jit_solution(8926895336405226867)
XLA Ops:
  0.0 0.0 copy-start
  0.0 0.9 reshape.70
  0.9 0.7 pad_add_fusion
  1.7 0.6 pad_bitcast_fusion.in_ref
  2.3 12.8 %shard_map.100 = s32[8,4,8,128]{3,2,1,0:T(8,128)} custom-call(s32[8,128]{1,0:T(8,128)} %pad_bitcast_fusion.in_ref), custom_call_target="tpu_custom_call" | custom-call | tf_op jit(solution)/shard_map/pallas_call | solution.py:78
  15.1 0.9 reshape.72
  16.1 0.1 slice.10
  16.2 0.1 reshape.73
  16.3 0.1 eq.25
  16.4 0.4 select_reduce_fusion
  16.8 0.2 fusion.6
  17.0 1.1 gather_fusion
  18.2 0.6 broadcast_6_live_ref.2.live_ref
  18.8 0.0 copy-start.1
  18.8 103.7 %shard_map.101 = bf16[256,1024]{1,0:T(8,128)(2,1)} custom-call(s32[8,2]{1,0:T(8,128)} %gather_fusion, s32[8,2]{1,0:T(8,128)} %broadcast_6_live_ref.2.live_ref, bf16[8,128,1024]{2,1,0:T(8,128)(2,1)} %bitcast.22, bf16[256,1024]{1,0:T(8,128)(2,1)} %grid_ref.1, bf16[1024,1024]{1,0:T(8,128)(2,1)} %wq_hbm.1, bf16[1024,1024]{1,0:T(8,128)(2,1)} %wk_hbm.1, ...), custom_call_target="tpu_custom_call" | custom-call | tf_op jit(solution)/shard_map/pallas_call | solution.py:224
  122.5 0.0 copy-done
  122.5 0.0 copy-done.1
  122.5 1.9 fusion.2
  124.4 5.8 %convolution_convert_fusion = bf16[256,3072]{1,0:T(8,128)(2,1)} fusion(bf16[1024,3072]{1,0:T(8,128)(2,1)} %param.18, bf16[256,1024]{1,0:T(8,128)(2,1)S(1)} %get-tuple-element.6, f32[256]{0:T(256)S(1)} %add_sqrt_fusion), kind=kOutput, calls=%fused_computation.1 | convolution fusion | flops 1612185600 | bytes 8389632 | tf_op jit(solution)/shard_map/dot_general | solution.py:447
  130.2 2.6 %copy.17 = bf16[256,3072]{0,1:T(8,128)(2,1)} copy(bf16[256,3072]{1,0:T(8,128)(2,1)} %convolution_convert_fusion) | data formatting | bytes 3145728 | tf_op jit(solution)/shard_map/convert_element_type | solution.py:447
  132.8 2.6 %copy.18 = bf16[256,8,384]{2,0,1:T(8,128)(2,1)} copy(bf16[256,8,384]{0,2,1:T(8,128)(2,1)} %bitcast.20) | data formatting | bytes 3145728 | tf_op jit(solution)/shard_map/reshape | solution.py:450
  135.3 0.0 copy-start.2
  135.4 61.2 %shard_map.102 = bf16[256,1024]{1,0:T(8,128)(2,1)} custom-call(bf16[8,256,384]{2,1,0:T(8,128)(2,1)} %bitcast.21), custom_call_target="tpu_custom_call" | custom-call | tf_op jit(solution)/shard_map/pallas_call | solution.py:375
  196.5 0.0 copy-done.2
  196.5 2.5 %fusion = bf16[256,1024]{1,0:T(8,128)(2,1)} fusion(bf16[256,1024]{1,0:T(8,128)(2,1)} %shard_map.102, bf16[1024,1024]{1,0:T(8,128)(2,1)S(1)} %copy-done.2, bf16[256,1024]{1,0:T(8,128)(2,1)S(1)} %get-tuple-element.6), kind=kOutput, calls=%fused_computation.6 | convolution fusion | flops 537657344 | bytes 3670016 | tf_op jit(solution)/shard_map/dot_general | solution.py:453
  (7 shorter events, 0.1 us)
Async XLA Ops:
  0.0 122.5 %copy-start = (bf16[1024,1024]{1,0:T(8,128)(2,1)S(1)}, bf16[1024,1024]{1,0:T(8,128)(2,1)}, u32[]{:S(2)}) copy-start(bf16[1024,1024]{1,0:T(8,128)(2,1)} %param.17) | copy-start | bytes 6291460
  18.8 103.7 %copy-start.1 = (bf16[256,1024]{1,0:T(8,128)(2,1)S(1)}, bf16[256,1024]{1,0:T(8,128)(2,1)}, u32[]{:S(2)}) copy-start(bf16[256,1024]{1,0:T(8,128)(2,1)} %grid_ref.1) | copy-start | bytes 1572868
  135.3 61.2 %copy-start.2 = (bf16[1024,1024]{1,0:T(8,128)(2,1)S(1)}, bf16[1024,1024]{1,0:T(8,128)(2,1)}, u32[]{:S(2)}) copy-start(bf16[1024,1024]{1,0:T(8,128)(2,1)} %param.19) | copy-start | bytes 6291460

commit v2 on v1

v2 whole, which is shorter than its diff:
```python
import functools
import math

import jax
import jax.numpy as jnp
from jax import lax
from jax.experimental import pallas as pl
from jax.experimental.pallas import tpu as pltpu
from jax.sharding import PartitionSpec as P

H = 16
SEG = 128

norm_eps = 1e-06
masked_score = -1e30
MESH = pl.DeviceIdType.MESH
VMEM_BYTES = 56 * 1024 * 1024


def rms_f32(widened):
    return widened / jnp.sqrt(jnp.mean(widened * widened, axis=-1, keepdims=True) + norm_eps)


def rms_rows(values):
    return rms_f32(values.astype(jnp.float32)).astype(jnp.bfloat16)


def stride_for(count):
    return 3 if math.gcd(3, count) == 1 else 1


def index_kernel(n_reg, n_seq, in_ref, out_ref, send_sem, recv_sem, send_sem2, recv_sem2):
    reg, seq = lax.axis_index("region"), lax.axis_index("seq")
    barrier = pltpu.get_barrier_semaphore()
    for k in range(1, n_reg):
        pl.semaphore_signal(
            barrier, inc=1, device_id=(lax.rem(reg + k, n_reg), seq), device_id_type=MESH
        )
    for k in range(1, n_seq):
        pl.semaphore_signal(
            barrier, inc=1, device_id=(reg, lax.rem(seq + k, n_seq)), device_id_type=MESH
        )
    out_ref[seq, reg] = in_ref[...]
    pl.semaphore_wait(barrier, n_reg + n_seq - 2)

    def over_region(k):
        return pltpu.make_async_remote_copy(
            src_ref=in_ref,
            dst_ref=out_ref.at[seq, reg],
            send_sem=send_sem.at[k],
            recv_sem=recv_sem.at[k],
            device_id=(lax.rem(reg + k, n_reg), seq),
            device_id_type=MESH,
        )

    for k in range(1, n_reg):
        over_region(k).start()
    for k in range(1, n_reg):
        over_region(k).wait()

    def over_seq(k):
        return pltpu.make_async_remote_copy(
            src_ref=out_ref.at[seq],
            dst_ref=out_ref.at[seq],
            send_sem=send_sem2.at[k],
            recv_sem=recv_sem2.at[k],
            device_id=(reg, lax.rem(seq + k, n_seq)),
            device_id_type=MESH,
        )

    for k in range(1, n_seq):
        over_seq(k).start()
    for k in range(1, n_seq):
        over_seq(k).wait()


def gather_indices(packed, n_reg, n_seq):
    return pl.pallas_call(
        functools.partial(index_kernel, n_reg, n_seq),
        out_shape=jax.ShapeDtypeStruct((n_seq, n_reg) + packed.shape, jnp.int32),
        in_specs=[pl.BlockSpec(memory_space=pltpu.VMEM)],
        out_specs=pl.BlockSpec(memory_space=pltpu.VMEM),
        scratch_shapes=[
            pltpu.SemaphoreType.DMA((n_reg,)),
            pltpu.SemaphoreType.DMA((n_reg,)),
            pltpu.SemaphoreType.DMA((n_seq,)),
            pltpu.SemaphoreType.DMA((n_seq,)),
        ],
        compiler_params=pltpu.CompilerParams(collective_id=0, has_side_effects=True),
    )(packed)


def group_bounds(n):
    return [(0, n)]


def region_phase(
    n, reg, me, heads, head_dim, rows, snd, out_ref,
    took, ks, vs, top, acc, made, got, send_sem, recv_sem, send_sem2, recv_sem2,
):
    stride = stride_for(n)

    def ahead(i):
        return lax.rem(me + stride * i, n)

    def behind(i):
        return lax.rem(me + (n * stride - stride * i), n)

    def outward(i):
        return pltpu.make_async_remote_copy(
            src_ref=snd.at[ahead(i)],
            dst_ref=took.at[i],
            send_sem=send_sem.at[i],
            recv_sem=recv_sem.at[i],
            device_id=(reg, ahead(i)),
            device_id_type=MESH,
        )

    def back(i):
        return pltpu.make_async_remote_copy(
            src_ref=made.at[i],
            dst_ref=got.at[me],
            send_sem=send_sem2.at[i],
            recv_sem=recv_sem2.at[i],
            device_id=(reg, behind(i)),
            device_id_type=MESH,
        )

    def back_in(i):
        return pltpu.make_async_remote_copy(
            src_ref=made.at[i],
            dst_ref=got.at[ahead(i)],
            send_sem=send_sem2.at[i],
            recv_sem=recv_sem2.at[i],
            device_id=(reg, ahead(i)),
            device_id_type=MESH,
        )

    def each(first, last, body):
        def step(i, carry):
            body(i)
            return carry

        lax.fori_loop(first, last, step, 0)

    each(1, n, lambda i: outward(i).start())
    for h in range(heads):
        vs[h, :, head_dim:] = jnp.ones((n * rows, head_dim), jnp.bfloat16)
    took[0] = snd[me]
    scale = 1.0 / math.sqrt(head_dim)

    def place(i):
        at = slice(i * rows, (i + 1) * rows)
        for h in range(heads):
            base = 3 * h * head_dim
            ks[h, at, :] = took[i, :, base + head_dim : base + 2 * head_dim]
            vs[h, at, :head_dim] = took[i, :, base + 2 * head_dim : base + 3 * head_dim]

    def scores_of(i, h, at, own=slice(None)):
        base = 3 * h * head_dim
        q = took[i, own, base : base + head_dim] * jnp.bfloat16(scale)
        return lax.dot_general(
            q, ks[h, at], (((1,), (1,)), ((), ())), preferred_element_type=jnp.float32
        )

    def finish(i, h, summed, own=slice(None)):
        made[i, own, h * head_dim : (h + 1) * head_dim] = (
            summed[:, :head_dim] / summed[:, head_dim:]
        ).astype(jnp.bfloat16)

    for low, high in group_bounds(n):
        for i in range(low, high):
            if i > 0:
                outward(i).wait_recv()
            place(i)
        last = high == n

        def older(i, low=low, high=high, last=last):
            at = slice(low * rows, high * rows)
            for h in range(heads):
                scores = scores_of(i, h, at)
                old = top[h * n + i]
                new = jnp.maximum(old, jnp.max(scores, axis=-1, keepdims=True))
                weights = jnp.exp((scores - new[:, :1]).astype(jnp.bfloat16))
                summed = jnp.dot(weights, vs[h, at], preferred_element_type=jnp.float32)
                summed = acc[h * n + i] * jnp.exp(old - new) + summed
                if last:
                    finish(i, h, summed)
                else:
                    acc[h * n + i] = summed
                    top[h * n + i] = new

        def fresh(i, low=low, high=high, last=last):
            at = slice(0, high * rows)
            parts = max(1, high * rows // 2048)
            for h in range(heads):
                for part in range(parts):
                    own = slice(part * rows // parts, (part + 1) * rows // parts)
                    scores = scores_of(i, h, at, own)
                    peak = jnp.max(scores, axis=-1, keepdims=True)
                    weights = jnp.exp((scores - peak).astype(jnp.bfloat16))
                    summed = jnp.dot(weights, vs[h, at], preferred_element_type=jnp.float32)
                    if last:
                        finish(i, h, summed, own)
                    else:
                        acc[h * n + i, own] = summed
                        top[h * n + i, own] = jnp.broadcast_to(peak, summed.shape)

        if last:
            def fresh_send(i, fresh=fresh):
                fresh(i)
                back(i).start()

            def older_send(i, older=older):
                older(i)
                back(i).start()

            each(max(low, 1), high, fresh_send)
            each(1, low, older_send)
            if low > 0:
                each(0, 1, older)
            else:
                each(0, 1, fresh)
        else:
            each(0, low, older)
            each(low, high, fresh)

    got[me] = made[0]
    each(1, n, lambda i: back_in(i).wait_recv())
    span = heads * head_dim
    for s in range(n):
        out_ref[:, s * span : (s + 1) * span] = got[s]
    each(1, n, lambda i: outward(i).wait_send())
    each(1, n, lambda i: back(i).wait_send())


def cross_kernel(
    n, blocks, pairs, head_dim, all_live,
    pick_ref, live_ref, scan_ref, grid_ref, wq_hbm, wk_hbm, wv_hbm, wm_hbm, wp_hbm,
    mixed_ref, out_ref,
    wq, wk, wv, wm, wp, send, recv, qm, ks, vs, top, sums, cross,
    snd, took, region_ks, region_vs, made, got,
    w_sem, send_sem, recv_sem, out_send, out_recv, back_send, back_recv,
):
    reg, me = lax.axis_index("region"), lax.axis_index("seq")
    stride = stride_for(n)
    weight_pairs = (
        (wq_hbm, wq), (wk_hbm, wk), (wv_hbm, wv), (wm_hbm, wm), (wp_hbm, wp)
    )
    loads = [
        pltpu.make_async_copy(src, dst, w_sem.at[i])
        for i, (src, dst) in enumerate(weight_pairs)
    ]
    for load in loads:
        load.start()
    barrier = pltpu.get_barrier_semaphore()
    for k in range(1, n):
        pl.semaphore_signal(
            barrier, inc=1, device_id=(reg, lax.rem(me + k, n)), device_id_type=MESH
        )
    pl.semaphore_wait(barrier, n - 1)

    def copy(i):
        return pltpu.make_async_remote_copy(
            src_ref=send.at[i],
            dst_ref=recv.at[i],
            send_sem=send_sem.at[i],
            recv_sem=recv_sem.at[i],
            device_id=(reg, lax.rem(me + stride * i, n)),
            device_id_type=MESH,
        )

    def stage(i, carry):
        for b in range(blocks):
            send[i, b * SEG : (b + 1) * SEG] = rms_rows(scan_ref[pick_ref[i, b]])
        copy(i).start()
        return carry

    lax.fori_loop(1, n, stage, 0)
    for b in range(blocks):
        recv[0, b * SEG : (b + 1) * SEG] = rms_rows(scan_ref[pick_ref[0, b]])

    rows = grid_ref.shape[0] // blocks
    width = 2 * head_dim
    low = lax.broadcasted_iota(jnp.int32, (rows, width), 1) < head_dim
    loads[0].wait()
    scale = 1.0 / math.sqrt(head_dim)
    queries = jnp.dot(rms_rows(grid_ref[...]), wq[...], preferred_element_type=jnp.float32)
    queries = queries.astype(jnp.bfloat16).astype(jnp.float32) * scale
    for b in range(blocks):
        for p in range(pairs):
            part = queries[b * rows : (b + 1) * rows, p * width : (p + 1) * width]
            j = b * pairs + p
            qm[j, :rows] = jnp.where(low, part, 0.0).astype(jnp.bfloat16)
            qm[j, rows:] = jnp.where(low, 0.0, part).astype(jnp.bfloat16)
    top[...] = jnp.full(top.shape, masked_score, jnp.float32)
    sums[...] = jnp.zeros(sums.shape, jnp.float32)
    for p in range(pairs):
        vs[p, :, width:] = jnp.ones((blocks * SEG, width), jnp.bfloat16)
    loads[1].wait()
    loads[2].wait()

    def process(i, carry):
        @pl.when(i > 0)
        def _():
            copy(i).wait_recv()

        arrived = recv[i]
        keys = jnp.dot(arrived, wk[...], preferred_element_type=jnp.float32).astype(jnp.bfloat16)
        for p in range(pairs):
            ks[p] = keys[:, p * width : (p + 1) * width]
        vals = jnp.dot(arrived, wv[...], preferred_element_type=jnp.float32).astype(jnp.bfloat16)
        for p in range(pairs):
            vs[p, :, :width] = vals[:, p * width : (p + 1) * width]

        for b in range(blocks):
            at = slice(b * SEG, (b + 1) * SEG)

            def attend(p, b, at):
                j = b * pairs + p
                scores = lax.dot_general(
                    qm[j], ks[p, at], (((1,), (1,)), ((), ())), preferred_element_type=jnp.float32
                )
                if not all_live:
                    scores = jnp.where(live_ref[i, b] > 0, scores, masked_score)
                old = top[j]
                new = jnp.maximum(old, jnp.max(scores, axis=-1, keepdims=True))
                weights = jnp.exp(scores - new).astype(jnp.bfloat16)
                factor = jnp.exp(old - new)
                factor = jnp.where(low, factor[:rows], factor[rows:])
                summed = jnp.dot(weights, vs[p, at], preferred_element_type=jnp.float32)
                sums[j, :rows] = sums[j, :rows] * factor + jnp.where(low, summed[:rows, :width], summed[rows:, :width])
                sums[j, rows:] = sums[j, rows:] * factor + jnp.where(
                    low, summed[:rows, width:], summed[rows:, width:]
                )
                top[j] = new

            def four(g, inner, b=b, at=at):
                for u in range(4):
                    attend(g * 4 + u, b, at)
                return inner

            lax.fori_loop(0, pairs // 4, four, 0)
        return carry

    lax.fori_loop(0, n, process, 0)
    for b in range(blocks):
        for p in range(pairs):
            j = b * pairs + p
            cross[b * rows : (b + 1) * rows, p * width : (p + 1) * width] = (
                sums[j, :rows] / sums[j, rows:]
            ).astype(jnp.bfloat16)

    loads[3].wait()
    loads[4].wait()
    mixed = (
        grid_ref[...].astype(jnp.float32)
        + jnp.dot(cross[...], wm[...], preferred_element_type=jnp.float32)
    ).astype(jnp.bfloat16)
    mixed_ref[...] = mixed
    normed = rms_rows(mixed)
    share = snd.shape[2]
    for d in range(n):
        snd[d] = jnp.dot(
            normed, wp[:, d * share : (d + 1) * share], preferred_element_type=jnp.float32
        ).astype(jnp.bfloat16)
    region_phase(
        n, reg, me, 2 * pairs // n, head_dim, grid_ref.shape[0], snd, out_ref, took, region_ks,
        region_vs, top, sums, made, got, out_send, out_recv, back_send, back_recv,
    )

    def finish(i, carry):
        copy(i).wait_send()
        return carry

    lax.fori_loop(1, n, finish, 0)


def both_attentions(pick, live, scan, grid_tokens, weights, n, blocks, all_live):
    rows, model = grid_tokens.shape
    head_dim = model // H
    pairs = H // 2
    width = 2 * head_dim
    block_rows = rows // blocks
    heads = H // n
    span = heads * head_dim
    vmem = pl.BlockSpec(memory_space=pltpu.VMEM)
    smem = pl.BlockSpec(memory_space=pltpu.SMEM)
    hbm = pl.BlockSpec(memory_space=pl.ANY)
    weight = pltpu.VMEM((model, model), jnp.bfloat16)
    return pl.pallas_call(
        functools.partial(cross_kernel, n, blocks, pairs, head_dim, all_live),
        out_shape=(jax.ShapeDtypeStruct((rows, model), jnp.bfloat16),) * 2,
        in_specs=[smem, smem, vmem, vmem] + [hbm] * 5,
        out_specs=(vmem, vmem),
        scratch_shapes=[
            weight,
            weight,
            weight,
            weight,
            pltpu.VMEM((model, 3 * model), jnp.bfloat16),
            pltpu.VMEM((n, blocks * SEG, model), jnp.bfloat16),
            pltpu.VMEM((n, blocks * SEG, model), jnp.bfloat16),
            pltpu.VMEM((blocks * pairs, 2 * block_rows, width), jnp.bfloat16),
            pltpu.VMEM((pairs, blocks * SEG, width), jnp.bfloat16),
            pltpu.VMEM((pairs, blocks * SEG, 2 * width), jnp.bfloat16),
            pltpu.VMEM((blocks * pairs, 2 * block_rows, SEG), jnp.float32),
            pltpu.VMEM((blocks * pairs, 2 * block_rows, width), jnp.float32),
            pltpu.VMEM((rows, model), jnp.bfloat16),
            pltpu.VMEM((n, rows, 3 * span), jnp.bfloat16),
            pltpu.VMEM((n, rows, 3 * span), jnp.bfloat16),
            pltpu.VMEM((heads, n * rows, head_dim), jnp.bfloat16),
            pltpu.VMEM((heads, n * rows, 2 * head_dim), jnp.bfloat16),
            pltpu.VMEM((n, rows, span), jnp.bfloat16),
            pltpu.VMEM((n, rows, span), jnp.bfloat16),
            pltpu.SemaphoreType.DMA((5,)),
        ] + [pltpu.SemaphoreType.DMA((n,))] * 6,
        compiler_params=pltpu.CompilerParams(
            collective_id=1, has_side_effects=True, vmem_limit_bytes=VMEM_BYTES
        ),
    )(pick, live, scan, grid_tokens, *weights)


def on_device(
    scan_tokens,
    grid_tokens,
    seg_slot,
    segment_lists,
    query_weight,
    key_weight,
    value_weight,
    mixer_weight,
    packed_weight,
    merged_weight,
):
    n_reg, n = lax.axis_size("region"), lax.axis_size("seq")
    reg, me = lax.axis_index("region"), lax.axis_index("seq")
    model_width = scan_tokens.shape[1]
    seg_local = scan_tokens.shape[0] // SEG
    blocks, overlap = segment_lists.shape

    flat = jnp.concatenate([seg_slot, segment_lists.reshape(-1)])
    used = flat.shape[0]
    tiles = -(-used // 1024)
    flat = jnp.pad(flat, (0, tiles * 1024 - used)).reshape(tiles * 8, 128)
    tables = gather_indices(flat, n_reg, n).reshape(n, n_reg, tiles * 1024)
    all_slots = jnp.swapaxes(tables[:, :, :seg_local], 0, 1).reshape(-1)
    lists = lax.dynamic_index_in_dim(tables, reg, axis=1, keepdims=False)
    lists = lists[:, seg_local:used].reshape(n, blocks, overlap)
    numbers = jnp.arange(all_slots.shape[0], dtype=jnp.int32)
    wanted = jnp.sum(jnp.where(lists[..., None] == numbers, all_slots, 0), axis=-1)
    wanted = wanted - reg * (n * seg_local)
    mine = wanted // seg_local == me
    pick = jnp.sum(jnp.where(mine, wanted % seg_local, 0), axis=-1)
    steps = stride_for(n) * jnp.arange(n, dtype=jnp.int32)
    targets = (me + steps) % n
    chosen = targets[:, None, None] == jnp.arange(n, dtype=jnp.int32)[None, :, None]
    pick = jnp.sum(jnp.where(chosen, pick[None], 0), axis=1)
    all_live = overlap == n
    if all_live:
        live = pick
    else:
        own = lax.dynamic_index_in_dim(wanted, me, axis=0, keepdims=False) // seg_local
        sources = (me - steps) % n
        live = jnp.any(own[None] == sources[:, None, None], axis=-1).astype(jnp.int32)

    weights = (query_weight, key_weight, value_weight, mixer_weight, packed_weight)
    mixed, returned = both_attentions(
        pick, live, scan_tokens.reshape(seg_local, SEG, model_width), grid_tokens, weights,
        n, blocks, all_live,
    )
    return (
        mixed.astype(jnp.float32)
        + jnp.dot(returned, merged_weight, preferred_element_type=jnp.float32)
    ).astype(jnp.bfloat16)


def solution(mesh):
    in_specs = (
        P(("region", "seq"), None),
        P(("region", "seq"), None),
        P(("region", "seq")),
        P(("region", "seq"), None),
        P(),
        P(),
        P(),
        P(),
        P(),
        P(),
    )
    out_specs = P(("region", "seq"), None)
    return jax.shard_map(
        on_device, mesh=mesh, in_specs=in_specs, out_specs=out_specs, check_vma=False
    )
```

time: 200 us -> 193 us (0.965)
  matrix products: 10.2 us -> 2.71 us
  Pallas kernels: 178 us -> 185 us
  local copies, waits for them, and re-layouts: 9.68 us -> 3.52 us
    dot_general x2 -> x0, matrix products: 7.66 us -> none  [the longest x1 5.79 us: on_device(): jnp.dot(rms_rows(mixed), packed_weight, preferred_element_type=jnp.float32)]
    pallas_call x2 -> x1, Pallas kernels: 165 us -> 172 us  [both_attentions(): pl.pallas_call(functools.partial(cross_kernel, n, blocks, pairs, head_dim...]
    convert_element_type x1 -> x0, local copies, waits for them, and re-layouts: 2.6 us -> none  [on_device(): jnp.dot(rms_rows(mixed), packed_weight, preferred_element_type=jnp.float32)]
    reshape x1 -> x0, local copies, waits for them, and re-layouts: 2.59 us -> none  [on_device(): packed.reshape(rows, n, -1)]
where the time goes in v2:
time: 193 us
  Pallas kernels  185 us (96%)
  local copies, waits for them, and re-layouts  3.52 us (2%)
  matrix products  2.71 us (1%)
    pallas_call x1, Pallas kernels, both_attentions(): pl.pallas_call(functools.partial(cross_kernel, n, blocks, pairs, head_dim...  172 us
    pallas_call x1, Pallas kernels, gather_indices(): pl.pallas_call(functools.partial(index_kernel, n_reg, n_seq), out_shape=j...  12.8 us

profile of v2, /device:TPU:2, one launch (start us, length us, event | category | flops | bytes accessed | tf_op | source)
XLA Modules:
  0.0 193.0 jit_solution(11016815703508245163)
XLA Ops:
  0.0 0.0 copy-start
  0.0 0.9 reshape.57
  0.9 0.7 pad_add_fusion
  1.7 0.1 iota_compare_fusion.1
  1.7 0.6 pad_bitcast_fusion.in_ref
  2.3 12.8 %shard_map.100 = s32[8,4,8,128]{3,2,1,0:T(8,128)} custom-call(s32[8,128]{1,0:T(8,128)} %pad_bitcast_fusion.in_ref), custom_call_target="tpu_custom_call" | custom-call | tf_op jit(solution)/shard_map/pallas_call | solution.py:78
  15.2 0.9 reshape.59
  16.2 0.1 slice.8
  16.3 0.1 reshape.60
  16.4 0.1 eq.46
  16.4 0.4 select_reduce_fusion
  16.9 0.2 fusion.1
  17.1 0.1 copy.17
  17.2 0.1 select_reduce_fusion.1
  17.3 0.7 copy.14.pick_ref.live_ref
  18.0 172.3 %shard_map.101 = (bf16[256,1024]{1,0:T(8,128)(2,1)}, bf16[256,1024]{1,0:T(8,128)(2,1)}) custom-call(s32[8,2]{1,0:T(8,128)} %copy.14.pick_ref.live_ref, s32[8,2]{1,0:T(8,128)} %copy.14.pick_ref.live_ref, bf16[8,128,1024]{2,1,0:T(8,128)(2,1)} %bitcast.13, bf16[256,1024]{1,0:T(8,128)(2,1)} %grid_ref.1, bf16[1024,1024]{1,0:T(8,128)(2,1)} %wq_hbm.1, ...), custom_call_target="tpu_custom_call" | custom-call | tf_op jit(solution)/shard_map/pallas_call | solution.py:391
  190.3 0.0 copy-done
  190.3 2.7 %fusion = bf16[256,1024]{1,0:T(8,128)(2,1)} fusion(bf16[256,1024]{1,0:T(8,128)(2,1)} %get-tuple-element.8, bf16[1024,1024]{1,0:T(8,128)(2,1)S(1)} %copy-done, bf16[256,1024]{1,0:T(8,128)(2,1)} %get-tuple-element.7), kind=kOutput, calls=%fused_computation.1 | convolution fusion | flops 537657344 | bytes 3670016 | tf_op jit(solution)/shard_map/dot_general | solution.py:474
  (5 shorter events, 0.1 us)
Async XLA Ops:
  0.0 190.3 %copy-start = (bf16[1024,1024]{1,0:T(8,128)(2,1)S(1)}, bf16[1024,1024]{1,0:T(8,128)(2,1)}, u32[]{:S(2)}) copy-start(bf16[1024,1024]{1,0:T(8,128)(2,1)} %param.19) | copy-start | bytes 6291460
